TPU v7x, 512 devices: a whole 4x8x8 slice. The times are simulated.
512 devices in a mesh: dp: 16 (over y_lo, z), seq: 32 (over y_hi, x, core).
Axes of the slice: x: 4, y: 8 (y_hi: 4, y_lo: 2; y = y_hi * 2 + y_lo), z: 8, core: 2. Of those that a mesh axis runs over, the one named last changes fastest.
Arguments:
- queries: bfloat16 [16, 4096, 512], P('dp', 'seq'), may hold values from -6 to 6
- keys: bfloat16 [16, 4096, 512], P('dp', 'seq'), may hold values from -6 to 6
- values: bfloat16 [16, 4096, 512], P('dp', 'seq'), may hold values from -6 to 6
- gates: bfloat16 [16, 4096, 512], P('dp', 'seq'), may hold values from -6 to 6
- out_proj: bfloat16 [512, 1024], replicated, may hold values from -0.25 to 0.25
- out_grad: bfloat16 [16, 4096, 1024], P('dp', 'seq'), may hold values from -6 to 6
- lengths: int32 [16, 4], P('dp'), may hold values from 1 to 2048, 4096 in all within a row
- rel_bias: float32 [4, 16], replicated, may hold values from -2 to 2
Outputs:
- projected: bfloat16 [16, 4096, 1024], P('dp', 'seq')
- query_grad: bfloat16 [16, 4096, 512], P('dp', 'seq')
- key_grad: bfloat16 [16, 4096, 512], P('dp', 'seq')
- value_grad: bfloat16 [16, 4096, 512], P('dp', 'seq')
- bias_grad: float32 [4, 16], replicated
Inputs may be any that keep to these rules, and one draw needn't show every extreme that they name: In every data row the 4 lengths sum to 4096 and the longest is exactly half of 4096.
All inputs are finite; a program needn't handle non-finite values.
Results may differ from a plain program's by a relative error of at most 0.0059.
Values may be sent and summed in bfloat16 or wider, within the bound.
A program may use at most 64 MiB of HBM per device.

v0:
```python
import math
import jax
import jax.numpy as jnp
from jax import lax
from jax.sharding import PartitionSpec as P

epsilon = 1e-05


def positions_and_segments(lengths_row, first_row, row_total):
    ends = jnp.cumsum(lengths_row)
    where_at = first_row + jnp.arange(row_total, dtype=jnp.int32)
    segment = jnp.sum((where_at[:, None] >= ends[None, :]).astype(jnp.int32), axis=1)
    return (where_at, segment)


def segment_bounds(lengths_row, segment_id):
    ends = jnp.cumsum(lengths_row)
    starts = ends - lengths_row
    picked = jnp.arange(lengths_row.shape[0], dtype=jnp.int32) == segment_id
    return (jnp.sum(jnp.where(picked, starts, 0)), jnp.sum(jnp.where(picked, ends, 0)))


def pair_scores(query_block, query_pos, query_seg, key_block, key_pos, key_seg, rel_bias):
    head_width = query_block.shape[2]
    products = jnp.einsum(
        "qhd,khd->hqk", query_block, key_block, preferred_element_type=jnp.float32
    )
    distance = query_pos[:, None] - key_pos[None, :]
    bucket = jnp.zeros(distance.shape, jnp.int32)
    for octave in range(15):
        bucket = bucket + (distance >= 2**octave).astype(jnp.int32)
    one_hot = (bucket[:, :, None] == jnp.arange(rel_bias.shape[1], dtype=jnp.int32)).astype(
        jnp.float32
    )
    shifted = jnp.einsum("hb,qkb->hqk", rel_bias, one_hot, precision=lax.Precision.HIGHEST)
    scores = products * head_width ** (-0.5) + shifted
    allowed = ((query_seg[:, None] == key_seg[None, :]) & (distance >= 0))[None]
    return (scores, allowed, one_hot)


def over_blocks(step_fn, live_fn, running, arrays, first_row):
    row_total = arrays[0].shape[0]
    block_rows = math.gcd(row_total, 512)
    block_count = row_total // block_rows
    stacked = tuple(
        (member.reshape((block_count, block_rows) + member.shape[1:]) for member in arrays)
    )

    def advance(partial_sum, element):
        block_index, pieces = element
        block_first = first_row + block_index * block_rows
        updated = lax.cond(
            live_fn(block_first, block_rows),
            lambda state: step_fn(state, pieces, block_first),
            lambda state: state,
            partial_sum,
        )
        return (updated, None)

    result, unused = lax.scan(advance, running, (jnp.arange(block_count, dtype=jnp.int32), stacked))
    return result


def shards(queries, keys, values, gates, out_proj, out_grad, lengths, rel_bias):
    heads = rel_bias.shape[0]
    tok_rows = queries.shape[1]
    feature_width = queries.shape[2]
    head_width = feature_width // heads
    own_queries = queries[0].reshape(tok_rows, heads, head_width)
    own_keys = keys[0].reshape(tok_rows, heads, head_width)
    own_values = values[0].reshape(tok_rows, heads, head_width)
    own_gates = gates[0].reshape(tok_rows, heads, head_width)
    lengths_row = lengths[0]
    own_first = lax.axis_index("seq") * tok_rows
    own_last = own_first + tok_rows - 1
    own_pos, own_seg = positions_and_segments(lengths_row, own_first, tok_rows)
    earliest_start, unused_end = segment_bounds(lengths_row, own_seg[0])
    unused_start, latest_end = segment_bounds(lengths_row, own_seg[tok_rows - 1])
    zero_heads = jnp.zeros((tok_rows, heads, head_width), jnp.float32)

    def keys_live(block_first, count):
        return (block_first <= own_last) & (block_first + count > earliest_start)

    def queries_live(block_first, count):
        return (block_first + count > own_first) & (block_first < latest_end)

    def forward_step(running, pieces, first_row):
        key_block, value_block = pieces
        key_pos, key_seg = positions_and_segments(lengths_row, first_row, key_block.shape[0])
        scores, allowed, one_hot = pair_scores(
            own_queries, own_pos, own_seg, key_block, key_pos, key_seg, rel_bias
        )
        weights = jnp.where(allowed, jax.nn.silu(scores), 0.0).astype(jnp.bfloat16)
        return running + jnp.einsum(
            "hqk,khd->qhd", weights, value_block, preferred_element_type=jnp.float32
        )

    all_keys, all_values = (
        lax.all_gather(own_keys, "seq", axis=0, tiled=True),
        lax.all_gather(own_values, "seq", axis=0, tiled=True),
    )
    mixed = over_blocks(forward_step, keys_live, zero_heads, (all_keys, all_values), 0)
    average = jnp.mean(mixed, axis=2, keepdims=True)
    centred = mixed - average
    variance = jnp.mean(centred * centred, axis=2, keepdims=True)
    inverse = lax.rsqrt(variance + epsilon)
    normed = centred * inverse
    gated = (
        (normed * own_gates.astype(jnp.float32))
        .astype(jnp.bfloat16)
        .reshape(tok_rows, feature_width)
    )
    projected = jnp.dot(gated, out_proj, preferred_element_type=jnp.float32).astype(jnp.bfloat16)
    gated_grad = jnp.einsum("te,ce->tc", out_grad[0], out_proj, preferred_element_type=jnp.float32)
    normed_grad = gated_grad.reshape(tok_rows, heads, head_width) * own_gates.astype(jnp.float32)
    mixed_grad = (
        normed_grad
        - jnp.mean(normed_grad, axis=2, keepdims=True)
        - normed * jnp.mean(normed_grad * normed, axis=2, keepdims=True)
    ) * inverse
    mixed_grad = mixed_grad.astype(jnp.bfloat16)

    def query_step(running, pieces, first_row):
        key_block, value_block = pieces
        key_pos, key_seg = positions_and_segments(lengths_row, first_row, key_block.shape[0])
        scores, allowed, one_hot = pair_scores(
            own_queries, own_pos, own_seg, key_block, key_pos, key_seg, rel_bias
        )
        sigmoid_s = jax.nn.sigmoid(scores)
        attn_grad = jnp.einsum(
            "qhd,khd->hqk", mixed_grad, value_block, preferred_element_type=jnp.float32
        )
        score_grad = jnp.where(
            allowed, attn_grad * sigmoid_s * (1.0 + scores * (1.0 - sigmoid_s)), 0.0
        )
        score_low = score_grad.astype(jnp.bfloat16)
        return running + jnp.einsum(
            "hqk,khd->qhd", score_low, key_block, preferred_element_type=jnp.float32
        )

    def key_step(running, pieces, first_row):
        key_total, value_total, bias_part = running
        query_block, grad_block = pieces
        query_pos, query_seg = positions_and_segments(lengths_row, first_row, query_block.shape[0])
        scores, allowed, one_hot = pair_scores(
            query_block, query_pos, query_seg, own_keys, own_pos, own_seg, rel_bias
        )
        sigmoid_s = jax.nn.sigmoid(scores)
        weights = jnp.where(allowed, scores * sigmoid_s, 0.0).astype(jnp.bfloat16)
        attn_grad = jnp.einsum(
            "qhd,khd->hqk", grad_block, own_values, preferred_element_type=jnp.float32
        )
        score_grad = jnp.where(
            allowed, attn_grad * sigmoid_s * (1.0 + scores * (1.0 - sigmoid_s)), 0.0
        )
        score_low = score_grad.astype(jnp.bfloat16)
        key_total = key_total + jnp.einsum(
            "hqk,qhd->khd", score_low, query_block, preferred_element_type=jnp.float32
        )
        value_total = value_total + jnp.einsum(
            "hqk,qhd->khd", weights, grad_block, preferred_element_type=jnp.float32
        )
        bias_terms = jnp.einsum("hqk,qkb->hb", score_grad, one_hot, precision=lax.Precision.HIGHEST)
        return (key_total, value_total, bias_part + bias_terms)

    first_row = jnp.int32(0)
    query_total = zero_heads
    key_total = zero_heads
    value_total = zero_heads
    bias_part = jnp.zeros(rel_bias.shape, jnp.float32)
    query_piece = lax.all_gather(own_queries, "seq", axis=0, tiled=True)
    grad_piece = lax.all_gather(mixed_grad, "seq", axis=0, tiled=True)
    key_piece = lax.all_gather(own_keys, "seq", axis=0, tiled=True)
    value_piece = lax.all_gather(own_values, "seq", axis=0, tiled=True)
    query_total = over_blocks(
        query_step, keys_live, query_total, (key_piece, value_piece), first_row
    )
    key_total, value_total, bias_part = over_blocks(
        key_step,
        queries_live,
        (key_total, value_total, bias_part),
        (query_piece, grad_piece),
        first_row,
    )
    query_total, key_total, value_total, bias_part = (
        query_total,
        key_total,
        value_total,
        bias_part,
    )
    bias_grad = lax.psum(bias_part, ("dp", "seq"))
    query_grad = query_total.reshape(1, tok_rows, feature_width).astype(jnp.bfloat16)
    key_grad = key_total.reshape(1, tok_rows, feature_width).astype(jnp.bfloat16)
    value_grad = value_total.reshape(1, tok_rows, feature_width).astype(jnp.bfloat16)
    return (projected[None], query_grad, key_grad, value_grad, bias_grad)


def solution(mesh):
    in_specs = (
        P("dp", "seq", None),
        P("dp", "seq", None),
        P("dp", "seq", None),
        P("dp", "seq", None),
        P(),
        P("dp", "seq", None),
        P("dp", None),
        P(),
    )
    out_specs = (
        P("dp", "seq", None),
        P("dp", "seq", None),
        P("dp", "seq", None),
        P("dp", "seq", None),
        P(),
    )
    return jax.shard_map(shards, mesh=mesh, in_specs=in_specs, out_specs=out_specs, check_vma=False)
```

profile of v0, /device:TPU:1, one launch (start us, length us, event | category | flops | bytes accessed | tf_op | source)
XLA Modules:
  0.0 500.8 jit_solution(6191673273034674706)
XLA Ops:
  7.2 1.7 copy.79
  14.4 1.7 copy.86
  16.8 2.7 fusion.98
  19.5 68.8 %all-gather.5.cloned.1.call-done = bf16[4096,4,128]{0,2,1:T(8,128)(2,1)} async-done(((bf16[128,4,128]{0,2,1:T(8,128)(2,1)}), bf16[4096,4,128]{0,2,1:T(8,128)(2,1)}) %all-gather.5.cloned.1.call-update) | async-done | bytes 4194320 | tf_op jit(solution)/shard_map/all_gather | solution.py:100
  88.3 6.4 %copy.103 = bf16[64,8,8,512]{3,2,1,0:T(8,128)(2,1)} copy(bf16[64,8,8,512]{3,1,2,0:T(8,128)(2,1)} %bitcast.164) | data formatting | bytes 8388608
  94.6 7.9 %copy.82 = bf16[8,512,4,128]{3,1,2,0:T(8,128)(2,1)} copy(bf16[8,512,4,128]{1,0,3,2:T(8,128)(2,1)} %bitcast.159) | data formatting | bytes 8388608
  102.6 58.8 %all-gather.7.cloned.1.call-done = bf16[4096,4,128]{0,2,1:T(8,128)(2,1)} async-done(((bf16[128,4,128]{0,2,1:T(8,128)(2,1)}), bf16[4096,4,128]{0,2,1:T(8,128)(2,1)}) %all-gather.7.cloned.1.call-update) | async-done | bytes 4194320 | tf_op jit(solution)/shard_map/all_gather | solution.py:101
  161.3 6.4 %copy.104 = bf16[64,8,8,512]{3,2,1,0:T(8,128)(2,1)} copy(bf16[64,8,8,512]{3,1,2,0:T(8,128)(2,1)} %bitcast.165) | data formatting | bytes 8388608
  167.7 7.9 %copy.84 = bf16[8,512,4,128]{3,1,2,0:T(8,128)(2,1)} copy(bf16[8,512,4,128]{1,0,3,2:T(8,128)(2,1)} %bitcast.160) | data formatting | bytes 8388608
  176.2 25.5 %while.44 = (s32[]{:T(128)}, f32[128,4,128]{2,0,1:T(8,128)S(1)}, s32[8]{0:T(128)}, s32[]{:T(128)}, s32[]{:T(128)}, /*index=5*/s32[128]{0:T(128)S(1)}, s32[4]{0:T...) while((s32[]{:T(128)}, f32[128,4,128]{2,0,1:T(8,128)S(1)}, ...), condition=%wide.region_8.9_spmd.clone, body=%wide.region_3.8_spmd.clone.sunk | while | flops 190978192 | bytes 7094895 | solution.py:61
  178.7 5.4 %conditional.10 = (f32[128,4,128]{2,0,1:T(8,128)S(1)}) conditional(s32[]{:T(128)} %convert_element_type.601, f32[128,4,128]{2,0,1:T(8,128)S(1)} %get-tuple-element.1113, (s32[128]{0:T(128)S(1)}, s32[]{:T(128)}, s32[4]{0:T(128)}, s32[]{:T(128)}, bf16[8,512,4,128]{3,1,2,0:T(8,128)(2,1)}, /*index=5*/s32[]{:T(128)}, bf16[128,4,128]{2,0,1:T(8,128)(2,1)S(1)}, ...), branch_computations={%region_4.4_spmd, %region_5.7_spmd} | conditional | flops 190978192 | bytes 7094084 | solution.py:53
  182.2 2.0 fusion.10
  203.6 1.7 multiply_convert_fusion
  206.2 1.7 copy.88
  209.1 27.4 %while.45 = (s32[]{:T(128)}, f32[128,4,128]{2,0,1:T(8,128)}, s32[8]{0:T(128)}, s32[]{:T(128)}, s32[]{:T(128)}, /*index=5*/s32[128]{0:T(128)S(1)}, s32[4]{0:T(128...) while((s32[]{:T(128)}, f32[128,4,128]{2,0,1:T(8,128)}, ...), condition=%wide.region_18.19_spmd.clone, body=%wide.region_13.18_spmd.clone.sunk | while | flops 259135632 | bytes 9847935 | solution.py:61
  211.6 7.6 %conditional.11 = (f32[128,4,128]{2,0,1:T(8,128)}) conditional(s32[]{:T(128)} %convert_element_type.602, f32[128,4,128]{2,0,1:T(8,128)} %get-tuple-element.1159, (s32[128]{0:T(128)S(1)}, s32[]{:T(128)}, s32[4]{0:T(128)}, s32[]{:T(128)}, bf16[8,512,4,128]{3,1,2,0:T(8,128)(2,1)}, /*index=5*/s32[]{:T(128)}, bf16[128,4,128]{2,0,1:T(8,128)(2,1)}, ...), branch_computations={%region_14.14_spmd, %region_15.17_spmd} | conditional | flops 259135632 | bytes 9847108 | solution.py:53
  216.4 2.8 fusion.38
  238.4 6.3 %copy.92 = bf16[4096,4,128]{2,0,1:T(8,128)(2,1)} copy(bf16[4096,4,128]{0,2,1:T(8,128)(2,1)} %all-gather.11.cloned.1.call-done) | data formatting | bytes 8388608 | tf_op jit(solution)/shard_map/all_gather | solution.py:172
  244.7 4.6 copy.95
  250.3 56.5 %all-gather.9.cloned.1.call-done = bf16[4096,4,128]{0,2,1:T(8,128)(2,1)} async-done(((bf16[128,4,128]{0,2,1:T(8,128)(2,1)}), bf16[4096,4,128]{0,2,1:T(8,128)(2,1)}) %all-gather.9.cloned.1.call-update) | async-done | bytes 4194320 | tf_op jit(solution)/shard_map/all_gather | solution.py:173
  306.8 6.4 %copy.105 = bf16[64,8,8,512]{3,2,1,0:T(8,128)(2,1)} copy(bf16[64,8,8,512]{3,1,2,0:T(8,128)(2,1)} %bitcast.163) | data formatting | bytes 8388608
  313.2 8.0 %copy.93 = bf16[8,512,4,128]{3,1,2,0:T(8,128)(2,1)} copy(bf16[8,512,4,128]{1,0,3,2:T(8,128)(2,1)} %bitcast.162) | data formatting | bytes 8388608
  321.2 64.0 %while.46 = (s32[]{:T(128)}, f32[128,4,128]{2,0,1:T(8,128)S(1)}, f32[128,4,128]{2,0,1:T(8,128)S(1)}, f32[4,16]{1,0:T(4,128)S(1)}, s32[8]{0:T(128)S(1)}, /*index=...) while((s32[]{:T(128)}, f32[128,4,128]{2,0,1:T(8,128)S(1)}, ...), condition=%wide.region_25.26_spmd.clone.clone, body=%wide.region_20.25_spmd.clone.clone.sunk | while | flops 379263168 | bytes 17516744 | solution.py:61
  323.1 12.2 %conditional.12 = ((f32[128,4,128]{2,0,1:T(8,128)S(1)}, f32[128,4,128]{2,0,1:T(8,128)S(1)}, f32[4,16]{1,0:T(4,128)S(1)})) conditional(s32[]{:T(128)} %convert_element_type.603, (f32[128,4,128]{2,0,1:T(8,128)S(1)}, f32[128,4,128]{2,0,1:T(8,128)S(1)}, f32[4,16]{1,0:T(4,128)S(1)}) %tuple.118, (s32[]{:T(128)}, s32[4]{0:T(128)S(1)}, s32[128]{0:T(128)S(1)}, ...), branch_computations={%region_21.21_spmd, %region_22.24_spmd} | conditional | flops 379263168 | bytes 17515868 | solution.py:53
  332.4 2.9 fusion.74
  337.2 12.2 %conditional.12 = ((f32[128,4,128]{2,0,1:T(8,128)S(1)}, f32[128,4,128]{2,0,1:T(8,128)S(1)}, f32[4,16]{1,0:T(4,128)S(1)})) conditional(s32[]{:T(128)} %convert_element_type.603, (f32[128,4,128]{2,0,1:T(8,128)S(1)}, f32[128,4,128]{2,0,1:T(8,128)S(1)}, f32[4,16]{1,0:T(4,128)S(1)}) %tuple.118, (s32[]{:T(128)}, s32[4]{0:T(128)S(1)}, s32[128]{0:T(128)S(1)}, ...), branch_computations={%region_21.21_spmd, %region_22.24_spmd} | conditional | flops 379263168 | bytes 17515868 | solution.py:53
  346.5 2.9 fusion.74
  351.3 12.2 %conditional.12 = ((f32[128,4,128]{2,0,1:T(8,128)S(1)}, f32[128,4,128]{2,0,1:T(8,128)S(1)}, f32[4,16]{1,0:T(4,128)S(1)})) conditional(s32[]{:T(128)} %convert_element_type.603, (f32[128,4,128]{2,0,1:T(8,128)S(1)}, f32[128,4,128]{2,0,1:T(8,128)S(1)}, f32[4,16]{1,0:T(4,128)S(1)}) %tuple.118, (s32[]{:T(128)}, s32[4]{0:T(128)S(1)}, s32[128]{0:T(128)S(1)}, ...), branch_computations={%region_21.21_spmd, %region_22.24_spmd} | conditional | flops 379263168 | bytes 17515868 | solution.py:53
  360.6 2.9 fusion.74
  365.4 12.2 %conditional.12 = ((f32[128,4,128]{2,0,1:T(8,128)S(1)}, f32[128,4,128]{2,0,1:T(8,128)S(1)}, f32[4,16]{1,0:T(4,128)S(1)})) conditional(s32[]{:T(128)} %convert_element_type.603, (f32[128,4,128]{2,0,1:T(8,128)S(1)}, f32[128,4,128]{2,0,1:T(8,128)S(1)}, f32[4,16]{1,0:T(4,128)S(1)}) %tuple.118, (s32[]{:T(128)}, s32[4]{0:T(128)S(1)}, s32[128]{0:T(128)S(1)}, ...), branch_computations={%region_21.21_spmd, %region_22.24_spmd} | conditional | flops 379263168 | bytes 17515868 | solution.py:53
  374.7 2.9 fusion.74
  387.0 107.3 %psum.7 = f32[4,16]{1,0:T(4,128)} all-reduce(f32[4,16]{1,0:T(4,128)S(1)} %get-tuple-element.505), channel_id=1, replica_groups=mesh['dp'=16,'seq'=32] {'dp','seq'}, use_global_device_ids=true, to_apply=%region_26.27 | all-reduce | flops 64 | bytes 512 | tf_op jit(solution)/shard_map/psum | solution.py:192
  (198 shorter events, 85.5 us)
Async XLA Ops:
  7.2 194.9 %copy-start = (bf16[512,1024]{1,0:T(8,128)(2,1)S(1)}, bf16[512,1024]{1,0:T(8,128)(2,1)}, u32[]{:S(2)}) copy-start(bf16[512,1024]{1,0:T(8,128)(2,1)} %param.24) | copy-start | bytes 3145732
  7.2 81.1 %all-gather.5.cloned.1.call-start = ((), (), s32[]{:S(2)}) async-start(), calls=%async_computation | async-start | bytes 4325376 | tf_op jit(solution)/shard_map/all_gather | solution.py:100
  9.0 152.3 %all-gather.7.cloned.1.call-start = ((), (), s32[]{:S(2)}) async-start(), calls=%async_computation.1 | async-start | bytes 4325376 | tf_op jit(solution)/shard_map/all_gather | solution.py:101
  10.7 227.6 %all-gather.11.cloned.1.call-start = ((), (), s32[]{:S(2)}) async-start(), calls=%async_computation.3 | async-start | bytes 4325376 | tf_op jit(solution)/shard_map/all_gather | solution.py:172
  12.5 294.3 %all-gather.9.cloned.1.call-start = ((), (), s32[]{:S(2)}) async-start(), calls=%async_computation.2 | async-start | bytes 4325376 | tf_op jit(solution)/shard_map/all_gather | solution.py:173
  167.7 8.5 %copy-start.4 = (f32[4,16]{1,0:T(4,128)S(1)}, f32[4,16]{1,0:T(4,128)}, u32[]{:S(2)}) copy-start(f32[4,16]{1,0:T(4,128)} %param.27) | copy-start | bytes 772
  201.7 3.6 copy-start.3
  201.7 4.4 copy-start.2
  313.2 8.0 %copy-start.5 = (bf16[128,4,128]{2,0,1:T(8,128)(2,1)S(1)}, bf16[128,4,128]{2,0,1:T(8,128)(2,1)}, u32[]{:S(2)}) copy-start(bf16[128,4,128]{2,0,1:T(8,128)(2,1)} %copy.94) | copy-start | bytes 393220
  313.2 8.0 %copy-start.6 = (s32[4]{0:T(128)S(1)}, s32[4]{0:T(128)}, u32[]{:S(2)}) copy-start(s32[4]{0:T(128)} %get-tuple-element.1271) | copy-start | bytes 52
  385.2 109.0 %copy-start.1 = (bf16[512,1024]{1,0:T(8,128)(2,1)S(1)}, bf16[512,1024]{1,0:T(8,128)(2,1)}, u32[]{:S(2)}) copy-start(bf16[512,1024]{1,0:T(8,128)(2,1)} %param.24) | copy-start | bytes 3145732
Sparse Core Ops, SparseCore 0:
  11.6 76.5 all-gather.4
  91.9 69.3 all-gather.6
  165.0 69.4 all-gather.10
  237.3 69.4 all-gather.8
where the time goes:
time: 504 us; the launch traced here: 501 us
  waiting for transfers between devices  184 us (37%)
  blocking collectives  107 us (21%)
  local copies, waits for them, and re-layouts  99.6 us (20%)
  matrix products  51.6 us (10%)
  loops' own time  30.7 us (6%)
  between operations  14 us (3%)
  other arithmetic  13.4 us (3%)
    psum x1, blocking collectives, shards(): bias_grad = lax.psum(bias_part, ('dp', 'seq'))  107 us
    all_gather x1, waiting for transfers between devices, shards(): lax.all_gather(own_keys, 'seq', axis=0, tiled=True)  68.8 us
    all_gather x1, waiting for transfers between devices, shards(): lax.all_gather(own_values, 'seq', axis=0, tiled=True)  58.8 us
    all_gather x1, waiting for transfers between devices, shards(): grad_piece = lax.all_gather(mixed_grad, 'seq', axis=0, tiled=True)  56.5 us
    unnamed x28, local copies, waits for them, and re-layouts  56.2 us
    another operation x3, loops' own time, over_blocks(): lax.scan(advance, running, (jnp.arange(block_count, dtype=jnp.int32), sta...  29.9 us
    dynamic_slice x24, local copies, waits for them, and re-layouts, over_blocks(): lax.scan(advance, running, (jnp.arange(block_count, dtype=jnp.int32), sta...  24.9 us
    dot_general x4, matrix products, key_step(): jnp.einsum('hqk,qkb->hb', score_grad, one_hot, precision=lax.Precision.HI...  11.5 us
  transfers between devices with their start and end apart: 4, of which 3 were waited for; matrix products, arithmetic and copies ran while one was open for 19% of the time, Pallas kernels for 0%

commit v1 on v0

--- a/solution.py
+++ b/solution.py
@@ -170,8 +170,11 @@
     value_total = zero_heads
     bias_part = jnp.zeros(rel_bias.shape, jnp.float32)
     query_piece = lax.all_gather(own_queries, "seq", axis=0, tiled=True)
-    grad_piece = lax.all_gather(mixed_grad, "seq", axis=0, tiled=True)
-    key_piece = lax.all_gather(own_keys, "seq", axis=0, tiled=True)
+    grad_piece, key_piece = jnp.split(
+        lax.all_gather(jnp.concatenate([mixed_grad, own_keys], axis=1), "seq", axis=0, tiled=True),
+        [mixed_grad.shape[1]],
+        axis=1,
+    )
     value_piece = lax.all_gather(own_values, "seq", axis=0, tiled=True)
     query_total = over_blocks(
         query_step, keys_live, query_total, (key_piece, value_piece), first_row

time: 504 us -> 609 us (1.21)
  the two profiles are of different devices: /device:TPU:1 before, /device:TPU:56 now
where the time goes in v1:
time: 609 us; the launch traced here: 607 us
  waiting for transfers between devices  212 us (35%)
  blocking collectives  145 us (24%)
  local copies, waits for them, and re-layouts  115 us (19%)
  matrix products  65.7 us (11%)
  loops' own time  33.4 us (5%)
  other arithmetic  20.7 us (3%)
  between operations  14 us (2%)
    psum x1, blocking collectives, shards(): bias_grad = lax.psum(bias_part, ('dp', 'seq'))  145 us
    all_gather x1, waiting for transfers between devices, shards(): lax.all_gather(jnp.concatenate([mixed_grad, own_keys], axis=1), 'seq', ax...  79.7 us
    unnamed x30, local copies, waits for them, and re-layouts  68.5 us
    all_gather x1, waiting for transfers between devices, shards(): lax.all_gather(own_keys, 'seq', axis=0, tiled=True)  63.9 us
    all_gather x1, waiting for transfers between devices, shards(): lax.all_gather(own_values, 'seq', axis=0, tiled=True)  58.8 us
    another operation x3, loops' own time, over_blocks(): lax.scan(advance, running, (jnp.arange(block_count, dtype=jnp.int32), sta...  32.5 us
    dynamic_slice x24, local copies, waits for them, and re-layouts, over_blocks(): lax.scan(advance, running, (jnp.arange(block_count, dtype=jnp.int32), sta...  19 us
    dot_general x12, matrix products, pair_scores(): jnp.einsum('hb,qkb->hqk', rel_bias, one_hot, precision=lax.Precision.HIGH...  15.3 us
  transfers between devices with their start and end apart: 4, of which 4 were waited for; matrix products, arithmetic and copies ran while one was open for 15% of the time, Pallas kernels for 0%

profile of v1, /device:TPU:56, one launch (start us, length us, event | category | flops | bytes accessed | tf_op | source)
XLA Modules:
  0.0 606.8 jit_solution(16409471446394818694)
XLA Ops:
  19.4 63.9 %all-gather.5.cloned.1.call-done = bf16[4096,4,128]{0,2,1:T(8,128)(2,1)} async-done(((bf16[128,4,128]{0,2,1:T(8,128)(2,1)}), bf16[4096,4,128]{0,2,1:T(8,128)(2,1)}) %all-gather.5.cloned.1.call-update) | async-done | bytes 4194320 | tf_op jit(solution)/shard_map/all_gather | solution.py:100
  83.2 6.4 %copy.105 = bf16[64,8,8,512]{3,2,1,0:T(8,128)(2,1)} copy(bf16[64,8,8,512]{3,1,2,0:T(8,128)(2,1)} %bitcast.172) | data formatting | bytes 8388608
  89.6 7.9 %copy.84 = bf16[8,512,4,128]{3,1,2,0:T(8,128)(2,1)} copy(bf16[8,512,4,128]{1,0,3,2:T(8,128)(2,1)} %bitcast.165) | data formatting | bytes 8388608
  97.5 58.8 %all-gather.7.cloned.1.call-done = bf16[4096,4,128]{0,2,1:T(8,128)(2,1)} async-done(((bf16[128,4,128]{0,2,1:T(8,128)(2,1)}), bf16[4096,4,128]{0,2,1:T(8,128)(2,1)}) %all-gather.7.cloned.1.call-update) | async-done | bytes 4194320 | tf_op jit(solution)/shard_map/all_gather | solution.py:101
  156.3 6.3 %copy.106 = bf16[64,8,8,512]{3,2,1,0:T(8,128)(2,1)} copy(bf16[64,8,8,512]{3,1,2,0:T(8,128)(2,1)} %bitcast.173) | data formatting | bytes 8388608
  162.6 7.9 %copy.86 = bf16[8,512,4,128]{3,1,2,0:T(8,128)(2,1)} copy(bf16[8,512,4,128]{1,0,3,2:T(8,128)(2,1)} %bitcast.166) | data formatting | bytes 8388608
  170.6 42.8 %while.44 = (s32[]{:T(128)}, f32[128,4,128]{2,0,1:T(8,128)S(1)}, s32[8]{0:T(128)S(1)}, s32[]{:T(128)}, s32[]{:T(128)}, /*index=5*/s32[128]{0:T(128)S(1)}, s32[4]...) while((s32[]{:T(128)}, f32[128,4,128]{2,0,1:T(8,128)S(1)}, ...), condition=%wide.region_8.9_spmd.clone, body=%wide.region_3.8_spmd.clone.sunk | while | flops 190978192 | bytes 7094887 | solution.py:61
  176.5 5.4 conditional.10
  183.9 5.4 conditional.10
  191.3 5.4 conditional.10
  198.6 5.4 conditional.10
  206.0 5.4 conditional.10
  219.5 9.8 %all-gather.11.cloned.1.call-done = bf16[4096,4,128]{0,2,1:T(8,128)(2,1)} async-done(((bf16[128,4,128]{0,2,1:T(8,128)(2,1)}), bf16[4096,4,128]{0,2,1:T(8,128)(2,1)}) %all-gather.11.cloned.1.call-update) | async-done | bytes 4194320 | tf_op jit(solution)/shard_map/all_gather | solution.py:172
  229.3 6.3 %copy.94 = bf16[4096,4,128]{2,0,1:T(8,128)(2,1)} copy(bf16[4096,4,128]{0,2,1:T(8,128)(2,1)} %all-gather.11.cloned.1.call-done) | data formatting | bytes 8388608 | tf_op jit(solution)/shard_map/all_gather | solution.py:172
  235.6 4.6 copy.97
  241.2 79.7 %all-gather.9.cloned.1.call-done = bf16[4096,8,128]{0,2,1:T(8,128)(2,1)} async-done(((bf16[128,8,128]{0,2,1:T(8,128)(2,1)}), bf16[4096,8,128]{0,2,1:T(8,128)(2,1)}) %all-gather.9.cloned.1.call-update) | async-done | bytes 8388624 | tf_op jit(solution)/shard_map/all_gather | solution.py:174
  320.9 5.2 fusion.100
  326.1 4.2 copy.108
  330.3 7.9 %copy.95 = bf16[8,512,4,128]{3,1,2,0:T(8,128)(2,1)} copy(bf16[8,512,4,128]{1,0,3,2:T(8,128)(2,1)} %bitcast.168) | data formatting | bytes 8388608
  339.5 50.3 %while.46 = (s32[]{:T(128)}, f32[128,4,128]{2,0,1:T(8,128)S(1)}, f32[128,4,128]{2,0,1:T(8,128)}, f32[4,16]{1,0:T(4,128)S(1)}, s32[8]{0:T(128)}, /*index=5*/s32[]...) while((s32[]{:T(128)}, f32[128,4,128]{2,0,1:T(8,128)S(1)}, ...), condition=%wide.region_25.26_spmd.clone.clone, body=%wide.region_20.25_spmd.clone.clone.sunk | while | flops 379263168 | bytes 19876116 | solution.py:61
  357.2 15.0 %conditional.12 = ((f32[128,4,128]{2,0,1:T(8,128)S(1)}, f32[128,4,128]{2,0,1:T(8,128)}, f32[4,16]{1,0:T(4,128)S(1)})) conditional(s32[]{:T(128)} %convert_element_type.603, (f32[128,4,128]{2,0,1:T(8,128)S(1)}, f32[128,4,128]{2,0,1:T(8,128)}, f32[4,16]{1,0:T(4,128)S(1)}) %tuple.119, (s32[]{:T(128)}, s32[4]{0:T(128)S(1)}, s32[128]{0:T(128)S(1)}, ...), branch_computations={%region_21.21_spmd, %region_22.24_spmd} | conditional | flops 379263168 | bytes 19875248 | solution.py:53
  364.8 2.9 fusion.74
  374.7 15.0 %conditional.12 = ((f32[128,4,128]{2,0,1:T(8,128)S(1)}, f32[128,4,128]{2,0,1:T(8,128)}, f32[4,16]{1,0:T(4,128)S(1)})) conditional(s32[]{:T(128)} %convert_element_type.603, (f32[128,4,128]{2,0,1:T(8,128)S(1)}, f32[128,4,128]{2,0,1:T(8,128)}, f32[4,16]{1,0:T(4,128)S(1)}) %tuple.119, (s32[]{:T(128)}, s32[4]{0:T(128)S(1)}, s32[128]{0:T(128)S(1)}, ...), branch_computations={%region_21.21_spmd, %region_22.24_spmd} | conditional | flops 379263168 | bytes 19875248 | solution.py:53
  392.4 145.2 %psum.7 = f32[4,16]{1,0:T(4,128)} all-reduce(f32[4,16]{1,0:T(4,128)S(1)} %get-tuple-element.505), channel_id=1, replica_groups=mesh['dp'=16,'seq'=32] {'dp','seq'}, use_global_device_ids=true, to_apply=%region_26.27 | all-reduce | flops 64 | bytes 512 | tf_op jit(solution)/shard_map/psum | solution.py:195
  537.6 6.4 %copy.107 = bf16[64,8,8,512]{3,2,1,0:T(8,128)(2,1)} copy(bf16[64,8,8,512]{3,1,2,0:T(8,128)(2,1)} %bitcast.170) | data formatting | bytes 8388608
  544.0 8.0 %copy.91 = bf16[8,512,4,128]{3,1,2,0:T(8,128)(2,1)} copy(bf16[8,512,4,128]{1,0,3,2:T(8,128)(2,1)} %bitcast.169) | data formatting | bytes 8388608
  552.0 47.0 %while.45 = (s32[]{:T(128)}, f32[128,4,128]{2,0,1:T(8,128)S(1)}, s32[8]{0:T(128)S(1)}, s32[]{:T(128)}, s32[]{:T(128)}, /*index=5*/s32[128]{0:T(128)S(1)}, s32[4]...) while((s32[]{:T(128)}, f32[128,4,128]{2,0,1:T(8,128)S(1)}, ...), condition=%wide.region_18.19_spmd.clone, body=%wide.region_13.18_spmd.clone.sunk | while | flops 259135632 | bytes 9847927 | solution.py:61
  558.0 6.2 %conditional.11 = (f32[128,4,128]{2,0,1:T(8,128)S(1)}) conditional(s32[]{:T(128)} %convert_element_type.602, f32[128,4,128]{2,0,1:T(8,128)S(1)} %get-tuple-element.1161, (s32[128]{0:T(128)S(1)}, s32[]{:T(128)}, s32[4]{0:T(128)S(1)}, s32[]{:T(128)}, bf16[8,512,4,128]{3,1,2,0:T(8,128)(2,1)}, /*index=5*/s32[]{:T(128)}, ...), branch_computations={%region_14.14_spmd, %region_15.17_spmd} | conditional | flops 259135632 | bytes 9847108 | solution.py:53
  566.2 6.2 %conditional.11 = (f32[128,4,128]{2,0,1:T(8,128)S(1)}) conditional(s32[]{:T(128)} %convert_element_type.602, f32[128,4,128]{2,0,1:T(8,128)S(1)} %get-tuple-element.1161, (s32[128]{0:T(128)S(1)}, s32[]{:T(128)}, s32[4]{0:T(128)S(1)}, s32[]{:T(128)}, bf16[8,512,4,128]{3,1,2,0:T(8,128)(2,1)}, /*index=5*/s32[]{:T(128)}, ...), branch_computations={%region_14.14_spmd, %region_15.17_spmd} | conditional | flops 259135632 | bytes 9847108 | solution.py:53
  574.4 6.2 %conditional.11 = (f32[128,4,128]{2,0,1:T(8,128)S(1)}) conditional(s32[]{:T(128)} %convert_element_type.602, f32[128,4,128]{2,0,1:T(8,128)S(1)} %get-tuple-element.1161, (s32[128]{0:T(128)S(1)}, s32[]{:T(128)}, s32[4]{0:T(128)S(1)}, s32[]{:T(128)}, bf16[8,512,4,128]{3,1,2,0:T(8,128)(2,1)}, /*index=5*/s32[]{:T(128)}, ...), branch_computations={%region_14.14_spmd, %region_15.17_spmd} | conditional | flops 259135632 | bytes 9847108 | solution.py:53
  582.6 6.2 %conditional.11 = (f32[128,4,128]{2,0,1:T(8,128)S(1)}) conditional(s32[]{:T(128)} %convert_element_type.602, f32[128,4,128]{2,0,1:T(8,128)S(1)} %get-tuple-element.1161, (s32[128]{0:T(128)S(1)}, s32[]{:T(128)}, s32[4]{0:T(128)S(1)}, s32[]{:T(128)}, bf16[8,512,4,128]{3,1,2,0:T(8,128)(2,1)}, /*index=5*/s32[]{:T(128)}, ...), branch_computations={%region_14.14_spmd, %region_15.17_spmd} | conditional | flops 259135632 | bytes 9847108 | solution.py:53
  590.8 6.2 %conditional.11 = (f32[128,4,128]{2,0,1:T(8,128)S(1)}) conditional(s32[]{:T(128)} %convert_element_type.602, f32[128,4,128]{2,0,1:T(8,128)S(1)} %get-tuple-element.1161, (s32[128]{0:T(128)S(1)}, s32[]{:T(128)}, s32[4]{0:T(128)S(1)}, s32[]{:T(128)}, bf16[8,512,4,128]{3,1,2,0:T(8,128)(2,1)}, /*index=5*/s32[]{:T(128)}, ...), branch_computations={%region_14.14_spmd, %region_15.17_spmd} | conditional | flops 259135632 | bytes 9847108 | solution.py:53
  (268 shorter events, 128.2 us)
Async XLA Ops:
  7.2 206.7 %copy-start = (bf16[512,1024]{1,0:T(8,128)(2,1)S(1)}, bf16[512,1024]{1,0:T(8,128)(2,1)}, u32[]{:S(2)}) copy-start(bf16[512,1024]{1,0:T(8,128)(2,1)} %param.24) | copy-start | bytes 3145732
  7.2 76.0 %all-gather.5.cloned.1.call-start = ((), (), s32[]{:S(2)}) async-start(), calls=%async_computation | async-start | bytes 4325376 | tf_op jit(solution)/shard_map/all_gather | solution.py:100
  9.0 147.3 %all-gather.7.cloned.1.call-start = ((), (), s32[]{:S(2)}) async-start(), calls=%async_computation.1 | async-start | bytes 4325376 | tf_op jit(solution)/shard_map/all_gather | solution.py:101
  10.7 218.6 %all-gather.11.cloned.1.call-start = ((), (), s32[]{:S(2)}) async-start(), calls=%async_computation.3 | async-start | bytes 4325376 | tf_op jit(solution)/shard_map/all_gather | solution.py:172
  12.5 308.5 %all-gather.9.cloned.1.call-start = ((), (), s32[]{:S(2)}) async-start(), calls=%async_computation.2 | async-start | bytes 8650752 | tf_op jit(solution)/shard_map/all_gather | solution.py:174
  162.6 8.0 %copy-start.7 = (f32[4,16]{1,0:T(4,128)S(1)}, f32[4,16]{1,0:T(4,128)}, u32[]{:S(2)}) copy-start(f32[4,16]{1,0:T(4,128)} %param.27) | copy-start | bytes 772
  162.6 8.0 %copy-start.9 = (s32[1,4]{1,0:T(1,128)S(1)}, s32[1,4]{1,0:T(1,128)}, u32[]{:S(2)}) copy-start(s32[1,4]{1,0:T(1,128)} %param.26) | copy-start | bytes 52
  213.4 3.0 copy-start.4
  213.5 4.5 copy-start.6
  357.2 0.7 copy-start.2
  362.1 0.6 copy-start.5
  369.8 2.4 copy-start.3
  374.8 0.7 copy-start.2
  379.6 0.6 copy-start.5
  387.4 2.4 copy-start.3
  544.0 8.0 %copy-start.8 = (bf16[128,4,128]{2,0,1:T(8,128)(2,1)S(1)}, bf16[128,4,128]{2,0,1:T(8,128)(2,1)}, u32[]{:S(2)}) copy-start(bf16[128,4,128]{2,0,1:T(8,128)(2,1)} %copy.90) | copy-start | bytes 393220
  599.0 1.3 copy-start.1
Sparse Core Ops, SparseCore 0:
  11.6 71.5 all-gather.4
  86.9 69.3 all-gather.6
  159.9 69.3 all-gather.10
  232.2 88.6 all-gather.8
